TPU v7x, 128 devices: a whole 4x4x4 slice. The times are simulated.
128 devices in a mesh: ctx: 8 (over z_lo, x), exp: 16 (over y, z_hi, core).
Axes of the slice: x: 4, y: 4, z: 4 (z_hi: 2, z_lo: 2; z = z_hi * 2 + z_lo), core: 2. Of those that a mesh axis runs over, the one named last changes fastest.
Arguments:
- tokens: bfloat16 [16384, 4096], P(('ctx', 'exp')), may hold values from -6 to 6
- block_order: int32 [128], replicated, may hold values from 0 to 127, each once
- attn_gain: bfloat16 [4096], replicated, may hold values from 0.25 to 1.75
- query_gain: bfloat16 [128], replicated, may hold values from 0.25 to 1.75
- key_gain: bfloat16 [128], replicated, may hold values from 0.25 to 1.75
- w_qkv: bfloat16 [4096, 768], P(None, 'exp'), may hold values from -0.09375 to 0.09375
- w_out: bfloat16 [512, 4096], P('exp'), may hold values from -0.25 to 0.25
- moe_gain: bfloat16 [4096], replicated, may hold values from 0.25 to 1.75
- router: bfloat16 [4096, 128], replicated, may hold values from -0.09375 to 0.09375
- routes: int32 [16384, 8], P(('ctx', 'exp')), may hold values from 0 to 127, all different within a row; in each aligned block of 128 rows (0 to 127, 128 to 255, ...) at most 9 rows name the same one
- w_gate_up: bfloat16 [128, 4096, 1536], P(('ctx', 'exp')), may hold values from -0.09375 to 0.09375
- w_down: bfloat16 [128, 768, 4096], P(('ctx', 'exp')), may hold values from -0.21875 to 0.21875
Outputs:
- layer_out: bfloat16 [16384, 4096], P(('ctx', 'exp'))
Inputs may be any that keep to these rules, and one draw needn't show every extreme that they name: Every block number appears once; index k of ctx+exp (ctx slowest) holds positions block_order[k] * 128 to block_order[k] * 128 + 127. `routes`: each token names 8 different experts. Among the rows of one device no expert is named more than 9 times, and in every draw some device names some expert exactly 9 times.
All inputs are finite; a program needn't handle non-finite values.
Results may differ from a plain program's by a relative error of at most 0.01.
Values may be sent and summed in bfloat16 or wider, within the bound.
No kernel may reach another device: no remote copies, remote signals or barrier semaphores. Data moves between devices by JAX's collectives and lax.ppermute only.
A program may use at most 128 MiB of HBM per device.

v0:
```python
import functools
import math

import jax
import jax.numpy as jnp
from jax import lax
from jax.experimental import pallas as pl
from jax.experimental.pallas import tpu as pltpu
from jax.sharding import PartitionSpec as P

rope_base = 1000000.0
GROUP = 8
VMEM_MB = 60
HIDDEN = -30000.0


def rms_scale(values, gain):
    widened = values.astype(jnp.float32)
    return (
        widened
        * lax.rsqrt(jnp.mean(widened * widened, axis=-1, keepdims=True) + 1e-06)
        * gain.astype(jnp.float32)
    )


def params(megabytes=VMEM_MB):
    return pltpu.CompilerParams(
        vmem_limit_bytes=megabytes * 1024 * 1024, dimension_semantics=("arbitrary",)
    )


def f32dot(a, b):
    return jnp.dot(a, b, preferred_element_type=jnp.float32)


def whole_block(shape):
    zeros = (0,) * len(shape)
    return pl.BlockSpec(shape, lambda *_: zeros, pipeline_mode=pl.Buffered(1))


def project_kernel(order_ref, *refs):
    ring = (len(refs) - 3) // 2
    x_refs, (near_ref, far_ref), out_refs, whole = (
        refs[:ring],
        refs[ring : ring + 2],
        refs[ring + 2 : -1],
        refs[-1],
    )
    half, columns = near_ref.shape[:2]
    rows = x_refs[0].shape[0]
    for e in range(2 * half):
        at = order_ref[e]
        near = near_ref[lax.rem(at, half)].astype(jnp.float32)
        far = far_ref[lax.rem(at, half)].astype(jnp.float32)
        whole[e * columns : (e + 1) * columns, :] = jnp.where(at < half, near, far).astype(
            jnp.bfloat16
        )
    x = jnp.concatenate([ref[...] for ref in x_refs], axis=0)
    out = lax.dot_general(
        x, whole[...], (((1,), (1,)), ((), ())), preferred_element_type=jnp.float32
    ).astype(jnp.bfloat16)
    for at, ref in enumerate(out_refs):
        ref[...] = out[at * rows : (at + 1) * rows]


def project(shares, near, far, order):
    rows, depth = shares[0].shape
    half, columns = near.shape[:2]
    out = jax.ShapeDtypeStruct((rows, 2 * half * columns), jnp.bfloat16)
    return pl.pallas_call(
        project_kernel,
        grid_spec=pltpu.PrefetchScalarGridSpec(
            num_scalar_prefetch=1,
            grid=(1,),
            in_specs=[whole_block(x.shape) for x in (*shares, near, far)],
            out_specs=[whole_block(out.shape)] * len(shares),
            scratch_shapes=[pltpu.VMEM((2 * half * columns, depth), jnp.bfloat16)],
        ),
        out_shape=[out] * len(shares),
        compiler_params=params(16),
        name="project",
    )(order, *shares, near, far)


def shape_kernel(heads, size, *refs):
    parts, (scale_ref, qgain_ref, kgain_ref, cos_ref, sin_ref, q_ref, kv_ref) = refs[:-7], refs[-7:]
    mixed = parts[0][...].astype(jnp.float32)
    for ref in parts[1:]:
        mixed = mixed + ref[...].astype(jnp.float32)
    mixed = mixed * scale_ref[...]
    half = size // 2

    def rope(values, gain):
        scale = lax.rsqrt(jnp.mean(values * values, axis=1, keepdims=True) + 1e-06)
        values = values * scale * gain.astype(jnp.float32)
        turned = jnp.concatenate([values[:, half:], values[:, :half]], axis=1)
        return values * cos_ref[...] + turned * sin_ref[...]

    for h in range(heads):
        part = slice(h * size, (h + 1) * size)
        q = rope(mixed[:, part], qgain_ref[...]) * (math.log2(math.e) / math.sqrt(size))
        q_ref[:, part] = q.astype(jnp.bfloat16)
    at = heads * size
    kv_ref[:, :size] = rope(mixed[:, at : at + size], kgain_ref[...]).astype(jnp.bfloat16)
    kv_ref[:, size:] = mixed[:, at + size :].astype(jnp.bfloat16)


def shape(parts, scale, query_gain, key_gain, cos, sin):
    rows, columns = parts[0].shape
    size = query_gain.shape[0]
    heads = columns // size - 2
    return pl.pallas_call(
        functools.partial(shape_kernel, heads, size),
        out_shape=[
            jax.ShapeDtypeStruct((rows, heads * size), jnp.bfloat16),
            jax.ShapeDtypeStruct((rows, 2 * size), jnp.bfloat16),
        ],
        compiler_params=pltpu.CompilerParams(vmem_limit_bytes=8 * 1024 * 1024),
        name="shape",
    )(*parts, scale, query_gain.reshape(1, -1), key_gain.reshape(1, -1), cos, sin)


def attend_kernel(heads, size, width, ring, last, first, *refs):
    q_refs, (kv_ref, hide_ref), refs = refs[:ring], refs[ring : ring + 2], refs[ring + 2 :]
    step = pl.program_id(0)
    index = step + first
    rows = q_refs[0].shape[0]
    length = kv_ref.shape[0]
    before_ref, (held, keys, values) = refs[0] if last else None, refs[-3:]
    out_refs = refs[1:-3] if last else refs[:-3]

    @pl.when(step == 0)
    def _():
        for at, ref in enumerate(q_refs):
            held[at] = ref[...]
        keys[:size, :] = kv_ref[:, :size].T
        keys[size:, :] = hide_ref[...]
        values[:, :size] = kv_ref[:, size:]
        values[:, size:] = jnp.ones((length, size), jnp.bfloat16)

    mark = lax.broadcasted_iota(jnp.int32, (rows, size), 1) == index
    mark = jnp.where(mark, 1.0, 0.0).astype(jnp.bfloat16)
    row = lax.broadcasted_iota(jnp.int32, (rows, width), 0)
    key = lax.broadcasted_iota(jnp.int32, (rows, width), 1)
    later = (key > row) & (key < rows) & (index == 0)
    totals = []
    for h in range(heads):
        q = jnp.concatenate([held[step, :, h * size : (h + 1) * size], mark], axis=1)
        if last:
            total = before_ref[0, h]
        else:
            total = jnp.zeros((rows, 2 * size), jnp.float32)
        for start in range(0, length, width):
            part = pl.ds(start, width)
            scores = f32dot(q, keys[:, part])
            if start == 0 and not last:
                scores = jnp.where(later, HIDDEN, scores)
            total = total + f32dot(jnp.exp2(scores).astype(jnp.bfloat16), values[part, :])
        totals.append(total)
    if not last:
        for h in range(heads):
            out_refs[0][0, h] = totals[h]
        return
    lane = lax.broadcasted_iota(jnp.int32, (rows, size), 1)
    sums = jnp.zeros((rows, size), jnp.float32)
    results = []
    for h, total in enumerate(totals):
        results.append(total[:, :size].astype(jnp.bfloat16))
        high = total[:, size:].astype(jnp.bfloat16).astype(jnp.float32)
        sums = jnp.where(lane == 2 * h, high, sums)
        sums = jnp.where(lane == 2 * h + 1, total[:, size:] - high, sums)
    packed = jnp.concatenate([*results, sums.astype(jnp.bfloat16)], axis=1)
    for at, ref in enumerate(out_refs):

        @pl.when(step == at)
        def _(ref=ref):
            ref[...] = packed


def attend(queries, key_values, hide, before, heads, size, first=0):
    rows, columns = queries[0].shape
    ring = len(queries)
    length = key_values.shape[0]
    last = before is not None
    totals = (heads, rows, 2 * size)
    totals_spec = pl.BlockSpec((1, *totals), lambda i: (i + first, 0, 0, 0))
    in_specs = [whole_block(x.shape) for x in (*queries, key_values)]
    in_specs.append(
        pl.BlockSpec((size, length), lambda i: (0, int(last)), pipeline_mode=pl.Buffered(1))
    )
    operands = [*queries, key_values, hide]
    if last:
        in_specs.append(totals_spec)
        operands.append(before)
        out = jax.ShapeDtypeStruct((rows, columns + size), jnp.bfloat16)
        out_specs, out_shape = [whole_block(out.shape)] * ring, [out] * ring
    else:
        out_specs = totals_spec
        out_shape = jax.ShapeDtypeStruct((ring, *totals), jnp.float32)
    return pl.pallas_call(
        functools.partial(attend_kernel, heads, size, 512, ring, last, first),
        grid=(ring,),
        in_specs=in_specs,
        out_specs=out_specs,
        scratch_shapes=[
            pltpu.VMEM((ring, rows, columns), jnp.bfloat16),
            pltpu.VMEM((2 * size, length), jnp.bfloat16),
            pltpu.VMEM((length, 2 * size), jnp.bfloat16),
        ],
        out_shape=out_shape,
        compiler_params=params(20),
        cost_estimate=pl.CostEstimate(
            flops=16 * heads * rows * ring * length * size,
            bytes_accessed=8000000,
            transcendentals=heads * rows * ring * length,
        ),
        name="attend",
    )(*operands)


def repeat_rows(values):
    rows = values.shape[0]
    row = lax.broadcasted_iota(jnp.int32, (rows * GROUP, rows), 0)
    column = lax.broadcasted_iota(jnp.int32, (rows * GROUP, rows), 1)
    copies = (lax.div(row, GROUP) == column).astype(jnp.bfloat16)
    return f32dot(copies, values)


def slots_kernel(routes_ref, pick_ref, last_ref, named_ref):
    fanout, tokens = routes_ref.shape
    count = named_ref.shape[0]
    expert = lax.broadcasted_iota(jnp.int32, (count, tokens), 0)
    named = jnp.zeros((count, tokens), jnp.float32)
    for j in range(fanout):
        named = named + jnp.where(routes_ref[j : j + 1, :] == expert, 1.0, 0.0)
    earlier = lax.broadcasted_iota(jnp.int32, (tokens, tokens), 0)
    later = lax.broadcasted_iota(jnp.int32, (tokens, tokens), 1)
    before = (earlier < later).astype(jnp.bfloat16)
    rank = f32dot(named.astype(jnp.bfloat16), before)
    code = named * (rank + 1.0)
    named_ref[...] = named
    last_ref[...] = (code == GROUP + 1.0).astype(jnp.bfloat16)
    spread = repeat_rows(code.astype(jnp.bfloat16))
    slot = lax.rem(lax.broadcasted_iota(jnp.int32, spread.shape, 0), GROUP) + 1
    pick_ref[...] = (spread == slot.astype(jnp.float32)).astype(jnp.bfloat16)


def slots(routes_t, count):
    fanout, tokens = routes_t.shape
    return pl.pallas_call(
        slots_kernel,
        out_shape=[
            jax.ShapeDtypeStruct((count * GROUP, tokens), jnp.bfloat16),
            jax.ShapeDtypeStruct((count, tokens), jnp.bfloat16),
            jax.ShapeDtypeStruct((count, tokens), jnp.float32),
        ],
        compiler_params=pltpu.CompilerParams(vmem_limit_bytes=VMEM_MB * 1024 * 1024),
        name="slots",
    )(routes_t)


def weigh_kernel(x_ref, router_ref, named_ref, pick_ref, last_ref, out_ref, out_last_ref):
    logits = lax.dot_general(
        router_ref[...], x_ref[...], (((0,), (1,)), ((), ())), preferred_element_type=jnp.float32
    )
    named = named_ref[...] > 0.5
    largest = jnp.max(jnp.where(named, logits, -jnp.inf), axis=0, keepdims=True)
    shares = jnp.where(named, jnp.exp(jnp.minimum(logits - largest, 0.0)), 0.0)
    shares = shares / jnp.sum(shares, axis=0, keepdims=True)
    shares = shares.astype(jnp.bfloat16)
    out_ref[...] = (repeat_rows(shares).astype(jnp.bfloat16) * pick_ref[...]).T
    out_last_ref[...] = (shares * last_ref[...]).T


def weigh(moe_in, router, named, pick, last):
    tokens = moe_in.shape[0]
    return pl.pallas_call(
        weigh_kernel,
        out_shape=[
            jax.ShapeDtypeStruct((tokens, pick.shape[0]), jnp.bfloat16),
            jax.ShapeDtypeStruct((tokens, last.shape[0]), jnp.bfloat16),
        ],
        compiler_params=pltpu.CompilerParams(vmem_limit_bytes=VMEM_MB * 1024 * 1024),
        name="weigh",
    )(moe_in, router, named, pick, last)


def fold(rows):
    count, features = rows.shape
    return rows.reshape(count, GROUP, features // GROUP).reshape(count * GROUP, features // GROUP)


def unfold(rows):
    count, piece = rows.shape
    return rows.reshape(count // GROUP, GROUP, piece).reshape(count // GROUP, GROUP * piece)


def finish_kernel(
    heads,
    size,
    features,
    *refs,
):
    parts_refs, refs = refs[:-12], refs[-12:]
    w_ref, x_ref, gain_ref, pick_ref, last_ref, resid_hbm, norm_hbm, out_ref = refs[:8]
    resid_ref, norm_ref, resid_sent, norm_sent = refs[8:]
    copies = (
        pltpu.make_async_copy(resid_ref, resid_hbm, resid_sent),
        pltpu.make_async_copy(norm_ref, norm_hbm, norm_sent),
    )

    @pl.when(pl.program_id(0) == 0)
    def _():
        summed = parts_refs[0][...].astype(jnp.float32)
        for ref in parts_refs[1:]:
            summed = summed + ref[...].astype(jnp.float32)
        base = heads * size
        attended = []
        for h in range(heads):
            at = base + 2 * h
            total = summed[:, at : at + 1] + summed[:, at + 1 : at + 2]
            attended.append((summed[:, h * size : (h + 1) * size] / total).astype(jnp.bfloat16))
        projected = f32dot(jnp.concatenate(attended, axis=1), w_ref[...])
        resid = x_ref[...].astype(jnp.float32) + projected
        resid_ref[...] = resid
        scale = lax.rsqrt(jnp.mean(resid * resid, axis=1, keepdims=True) + 1e-06)
        norm_ref[...] = (resid * scale * gain_ref[...].astype(jnp.float32)).astype(jnp.bfloat16)
        for copy in copies:
            copy.start()

    out_ref[:, :features] = f32dot(pick_ref[...], norm_ref[:, :features]).astype(jnp.bfloat16)
    out_ref[:, features:] = fold(f32dot(last_ref[...], norm_ref[...]).astype(jnp.bfloat16))

    @pl.when(pl.program_id(0) == pl.num_programs(0) - 1)
    def _():
        for copy in copies:
            copy.wait()


def finish(parts, w_out, tokens, gain, pick, last, heads, size, features):
    rows, count = pick.shape[0], last.shape[0]
    wide = features + tokens.shape[1] // GROUP
    blocks = 4
    return pl.pallas_call(
        functools.partial(finish_kernel, heads, size, features),
        grid=(blocks,),
        in_specs=[
            *(whole_block(x.shape) for x in parts),
            whole_block(w_out.shape),
            whole_block(tokens.shape),
            whole_block((1, gain.shape[0])),
            pl.BlockSpec((rows // blocks, pick.shape[1]), lambda i: (i, 0)),
            pl.BlockSpec((count // blocks, pick.shape[1]), lambda i: (i, 0)),
        ],
        out_specs=[
            pl.BlockSpec(memory_space=pl.ANY),
            pl.BlockSpec(memory_space=pl.ANY),
            pl.BlockSpec((rows // blocks, wide), lambda i: (i, 0)),
        ],
        scratch_shapes=[
            pltpu.VMEM(tokens.shape, jnp.float32),
            pltpu.VMEM(tokens.shape, jnp.bfloat16),
            pltpu.SemaphoreType.DMA(()),
            pltpu.SemaphoreType.DMA(()),
        ],
        out_shape=[
            jax.ShapeDtypeStruct(tokens.shape, jnp.float32),
            jax.ShapeDtypeStruct(tokens.shape, jnp.bfloat16),
            jax.ShapeDtypeStruct((rows, wide), jnp.bfloat16),
        ],
        compiler_params=params(57),
        name="finish",
    )(*parts, w_out, tokens, gain.reshape(1, -1), pick, last)


def dispatch_kernel(x_ref, pick_ref, out_ref):
    out_ref[...] = f32dot(pick_ref[...], x_ref[...]).astype(jnp.bfloat16)


def dispatch(normed, pick, chunk, features):
    rows, tokens = pick.shape
    blocks = 4
    return pl.pallas_call(
        dispatch_kernel,
        grid=(blocks,),
        in_specs=[
            pl.BlockSpec((tokens, features), lambda i: (0, chunk)),
            pl.BlockSpec((rows // blocks, tokens), lambda i: (i, 0)),
        ],
        out_specs=pl.BlockSpec((rows // blocks, features), lambda i: (i, 0)),
        out_shape=jax.ShapeDtypeStruct((rows, features), jnp.bfloat16),
        compiler_params=params(),
        cost_estimate=pl.CostEstimate(
            flops=4 * rows * tokens * features, bytes_accessed=4 * rows * features, transcendentals=0
        ),
        name="dispatch",
    )(normed, pick)


def gated(gate_up):
    hidden = gate_up.shape[1] // 2
    gate = gate_up[:, :hidden]
    return (gate / (1.0 + jnp.exp(-gate)) * gate_up[:, hidden:]).astype(jnp.bfloat16)


def up_kernel(features, x_ref, wu_ref, wd_ref, out_ref, ninth_ref, last):
    index = pl.program_id(0)
    lasts = x_ref.shape[0] // GROUP
    out_ref[...] = f32dot(x_ref[:, :features], wu_ref[0, :features, :])
    last[pl.ds(pl.multiple_of(index * lasts, lasts), lasts), :] = unfold(x_ref[:, features:])

    @pl.when(index == pl.num_programs(0) - 1)
    def _():
        active = gated(f32dot(last[...], wu_ref[0]))
        ninth_ref[...] = fold(f32dot(active, wd_ref[0]).astype(jnp.bfloat16))


def up_first(received, w_up, w_down, features):
    rows, wide = received.shape
    columns = w_up.shape[2]
    width = w_down.shape[2]
    blocks = 4
    return pl.pallas_call(
        functools.partial(up_kernel, features),
        grid=(blocks,),
        in_specs=[
            pl.BlockSpec((rows // blocks, wide), lambda i: (i, 0)),
            whole_block(w_up.shape),
            whole_block(w_down.shape),
        ],
        out_specs=[
            pl.BlockSpec((rows // blocks, columns), lambda i: (i, 0)),
            pl.BlockSpec((rows, width // GROUP), lambda i: (0, 0)),
        ],
        out_shape=[
            jax.ShapeDtypeStruct((rows, columns), jnp.float32),
            jax.ShapeDtypeStruct((rows, width // GROUP), jnp.bfloat16),
        ],
        scratch_shapes=[pltpu.VMEM((rows // GROUP, width), jnp.bfloat16)],
        compiler_params=params(),
        cost_estimate=pl.CostEstimate(
            flops=2 * rows * features * columns, bytes_accessed=20000000, transcendentals=0
        ),
        name="up_first",
    )(received, w_up, w_down)


def expert_kernel(x_ref, wu_ref, partial_ref, ninth_ref, wd_hbm, out_ref, wd, arrived):
    index = pl.program_id(0)
    copy = pltpu.make_async_copy(wd_hbm.at[0], wd, arrived)

    @pl.when(index == 0)
    def _():
        copy.start()

    active = gated(partial_ref[...] + f32dot(x_ref[...], wu_ref[0]))

    @pl.when(index == 0)
    def _():
        copy.wait()

    width = wd.shape[1]
    out_ref[:, :width] = f32dot(active, wd[...]).astype(jnp.bfloat16)
    out_ref[:, width:] = ninth_ref[...]


def expert(received, w_up, partial, ninth, w_down, chunk):
    rows, features = received.shape
    columns = w_up.shape[2]
    hidden, width = w_down.shape[1:]
    blocks = 4
    out_wide = width + width // GROUP
    return pl.pallas_call(
        expert_kernel,
        grid=(blocks,),
        in_specs=[
            pl.BlockSpec((rows // blocks, features), lambda i: (i, 0)),
            pl.BlockSpec(
                (1, features, columns), lambda i: (0, chunk, 0), pipeline_mode=pl.Buffered(1)
            ),
            pl.BlockSpec((rows // blocks, columns), lambda i: (i, 0)),
            pl.BlockSpec((rows // blocks, width // GROUP), lambda i: (i, 0)),
            pl.BlockSpec(memory_space=pl.ANY),
        ],
        out_specs=pl.BlockSpec((rows // blocks, out_wide), lambda i: (i, 0)),
        out_shape=jax.ShapeDtypeStruct((rows, out_wide), jnp.bfloat16),
        scratch_shapes=[pltpu.VMEM((hidden, width), jnp.bfloat16), pltpu.SemaphoreType.DMA(())],
        compiler_params=params(55),
        cost_estimate=pl.CostEstimate(
            flops=2 * rows * (features * columns + hidden * width),
            bytes_accessed=30000000,
            transcendentals=0,
        ),
        name="expert",
    )(received, w_up, partial, ninth, w_down)


def combine_kernel(x_ref, ninth_ref, w_ref, wlast_ref, resid_ref, out_ref, last):
    width = resid_ref.shape[1]
    index = pl.program_id(0)

    @pl.when(index == 0)
    def _():
        last[...] = unfold(ninth_ref[...])

    own = last[:, pl.ds(pl.multiple_of(index * width, width), width)]
    added = f32dot(w_ref[...], x_ref[...]) + f32dot(wlast_ref[...], own)
    out_ref[...] = (resid_ref[...] + added).astype(jnp.bfloat16)


def combine(returned, weights, last_weights, resid):
    rows = returned.shape[0]
    tokens, features = resid.shape
    count = last_weights.shape[1]
    blocks = 2
    width = features // blocks
    return pl.pallas_call(
        combine_kernel,
        grid=(blocks,),
        in_specs=[
            pl.BlockSpec((rows, width), lambda i: (0, i)),
            pl.BlockSpec(
                (rows, features // GROUP), lambda i: (0, GROUP), pipeline_mode=pl.Buffered(1)
            ),
            whole_block((tokens, rows)),
            whole_block((tokens, count)),
            pl.BlockSpec((tokens, width), lambda i: (0, i)),
        ],
        out_specs=pl.BlockSpec((tokens, width), lambda i: (0, i)),
        out_shape=jax.ShapeDtypeStruct((tokens, features), jnp.bfloat16),
        scratch_shapes=[pltpu.VMEM((count, features), jnp.bfloat16)],
        compiler_params=params(),
        name="combine",
    )(returned, returned, weights, last_weights, resid)


def on_device(
    tokens,
    block_order,
    attn_gain,
    query_gain,
    key_gain,
    w_qkv,
    w_out,
    moe_gain,
    router,
    routes,
    w_gate_up,
    w_down,
):
    rows, model_width = tokens.shape
    size = query_gain.shape[0]
    ctx_size, exp_size = lax.axis_size("ctx"), lax.axis_size("exp")
    ctx_at, exp_at = lax.axis_index("ctx"), lax.axis_index("exp")
    ring = 4
    inner = exp_size // ring
    x_at, z_lo = ctx_at % ring, ctx_at // ring
    y_at, z_hi, core = exp_at // inner, exp_at // 2 % 2, exp_at % 2

    def device(z_lo, x, y, z_hi, core):
        return (z_lo * ring + x) * exp_size + y * inner + z_hi * 2 + core

    def bring(value, z_lo=0, x=0, y=0, z_hi=0, core=0):
        pairs = []
        for at in range(ctx_size * exp_size):
            c, e = at // exp_size, at % exp_size
            source = device(
                c // ring ^ z_lo,
                (c - x) % ring,
                (e // inner - y) % ring,
                e // 2 % 2 ^ z_hi,
                e % 2 ^ core,
            )
            pairs.append((source, at))
        return lax.ppermute(value, ("ctx", "exp"), pairs)

    def along_y(value):
        return jnp.concatenate([value] + [bring(value, y=k) for k in range(1, ring)])

    def along_x(values, step):
        return [values[0]] + [bring(values[k], x=step * k) for k in range(1, ring)]

    relative = jnp.arange(exp_size, dtype=jnp.int32)
    piece_of = (
        (core + relative) % 2 * (2 * ring)
        + (y_at - relative // inner) % ring * 2
        + (z_hi + relative // 2) % 2
    )
    relative = jnp.arange(2 * exp_size, dtype=jnp.int32)
    key_devices = device(
        (z_lo + relative) % 2,
        x_at,
        (y_at - relative // 4) % ring,
        (z_hi + relative // 2) % 2,
        (core + relative // (4 * ring)) % 2,
    )
    steps = jnp.arange(ring, dtype=jnp.int32)
    query_devices = device(z_lo, (x_at - steps) % ring, y_at, z_hi, core)

    def block_numbers(devices):
        every = jnp.arange(block_order.shape[0], dtype=jnp.int32)
        return jnp.sum(
            jnp.where(devices[:, None] == every[None, :], block_order[None, :], 0), axis=1
        )

    k_blocks = block_numbers(key_devices)
    q_blocks = block_numbers(query_devices)
    own_pos = q_blocks[0] * rows + jnp.arange(rows, dtype=jnp.int32)
    hide = jnp.repeat(
        jnp.where(k_blocks[None, :] > q_blocks[:, None], HIDDEN, 0.0), rows, axis=1
    )
    hide = jnp.pad(hide, ((0, size - ring), (0, 0))).astype(jnp.bfloat16)

    depth = model_width // ring
    widened = tokens.astype(jnp.float32)
    row_scale = lax.rsqrt(jnp.mean(widened * widened, axis=1, keepdims=True) + 1e-06)
    gained = (widened * attn_gain.astype(jnp.float32)).astype(jnp.bfloat16)
    w_share = lax.dynamic_slice_in_dim(w_qkv.T, x_at * depth, depth, 1)
    other, gained = lax.optimization_barrier((bring(w_share, z_hi=1), gained))
    near = along_y(jnp.stack([w_share, other]))
    shares = along_x(
        [
            lax.dynamic_slice_in_dim(gained, (x_at + k) % ring * depth, depth, 1)
            for k in range(ring)
        ],
        1,
    )
    near, shares = lax.optimization_barrier((near, shares))
    far = bring(near, core=1)
    w_out_all = lax.all_gather(w_out, "exp", axis=0, tiled=True)
    shares = project(shares, near, far, piece_of)
    shares, routes = lax.optimization_barrier((shares, routes))
    count = router.shape[1]
    pick, pick_last, named = slots(routes.T, count)
    half = size // 2
    freqs = jnp.exp(
        -math.log(rope_base) * jnp.arange(half, dtype=jnp.float32) * 2.0 / size
    )
    angles = own_pos.astype(jnp.float32)[:, None] * freqs[None, :]
    cos, sin = jnp.cos(angles), jnp.sin(angles)
    cos = jnp.concatenate([cos, cos], axis=1)
    sin = jnp.concatenate([-sin, sin], axis=1)
    parts = along_x(shares, -1)
    parts, pick, pick_last, named, hide, cos, sin = lax.optimization_barrier(
        (parts, pick, pick_last, named, hide, cos, sin)
    )
    heads = parts[0].shape[1] // size - 2
    queries, key_values = shape(parts, row_scale, query_gain, key_gain, cos, sin)
    others = [
        bring(key_values, z_lo=1),
        bring(key_values, z_hi=1),
        bring(key_values, z_lo=1, z_hi=1),
    ]
    others, left, right = lax.optimization_barrier(
        (others, bring(queries, x=1), bring(queries, x=ring - 1))
    )
    near = along_y(jnp.stack([key_values, *others])).reshape(-1, 2 * size)
    near, across = lax.optimization_barrier((near, bring(queries, x=2)))
    queries = [queries, left, across, right]
    far = bring(near, core=1)
    totals = attend(queries, near, hide, None, heads, size)
    others = attend(queries[1:], far, hide, totals, heads, size, 1)
    own = attend(queries[:1], far, hide, totals, heads, size)
    parts = along_x([*own, *others], -1)
    main = model_width // 4 * 3
    rest = model_width - main
    resid, moe_in, outgoing = finish(
        parts, w_out_all, tokens, moe_gain, pick, pick_last, heads, size, main
    )

    def exchange(x):
        wide = x.shape[1]
        x = lax.all_to_all(
            x.reshape(count, GROUP, wide), ("ctx", "exp"), split_axis=0, concat_axis=0, tiled=True
        )
        return x.reshape(count * GROUP, wide)

    first = exchange(outgoing)
    second = exchange(dispatch(moe_in, pick, main // rest, rest))
    first, moe_in = lax.optimization_barrier((first, moe_in))
    weights, last_weights = weigh(moe_in, router, named, pick, pick_last)
    partial, ninth = up_first(first, w_gate_up, w_down, main)
    returned = exchange(expert(second, w_gate_up, partial, ninth, w_down, main // rest))
    return combine(returned, weights, last_weights, resid)


def solution(mesh):
    return jax.shard_map(
        on_device,
        mesh=mesh,
        in_specs=(
            P(("ctx", "exp"), None),
            P(),
            P(),
            P(),
            P(),
            P(None, "exp"),
            P("exp", None),
            P(),
            P(),
            P(("ctx", "exp"), None),
            P(("ctx", "exp"), None, None),
            P(("ctx", "exp"), None, None),
        ),
        out_specs=P(("ctx", "exp"), None),
        check_vma=False,
    )
```

profile of v0, /device:TPU:41, one launch (start us, length us, event | category | flops | bytes accessed | tf_op | source)
XLA Modules:
  0.0 419.4 jit_solution(7893114761448144965)
XLA Ops:
  7.3 0.9 dynamic-slice_bitcast_fusion.1
  8.2 2.7 collective-permute-start
  11.6 0.8 select_reduce_fusion.1
  12.5 0.8 select_reduce_fusion
  13.4 0.9 constant_dynamic-update-slice_fusion.4
  14.3 1.6 fusion.1
  16.2 2.3 collective-permute-start.2
  18.5 1.6 collective-permute-start.1
  20.2 2.5 collective-permute-start.6
  23.3 7.3 %collective-permute-done.1 = bf16[2,48,1024]{2,1,0:T(8,128)(2,1)S(1)} collective-permute-done((bf16[2,48,1024]{2,1,0:T(8,128)(2,1)S(1)}, bf16[2,48,1024]{2,1,0:T(8,128)(2,1)S(1)}, u32[]{:S(2)}, u32[]{:S(2)}) %collective-permute-start.1) | collective-permute-done | bytes 196640 | tf_op jit(solution)/shard_map/ppermute | solution.py:575
  30.6 1.2 collective-permute-start.4
  31.9 6.6 %collective-permute-done.4.refs_1_ = bf16[128,1024]{1,0:T(8,128)(2,1)S(1)} collective-permute-done((bf16[128,1024]{1,0:T(8,128)(2,1)S(1)}, bf16[128,1024]{1,0:T(8,128)(2,1)S(1)}, u32[]{:S(2)}, u32[]{:S(2)}) %collective-permute-start.4) | collective-permute-done | bytes 262176 | tf_op jit(solution)/shard_map/ppermute | solution.py:575
  38.5 2.0 collective-permute-start.7
  41.0 1.4 collective-permute-done.7.refs_5_
  42.4 1.6 project.1
  44.0 1.4 collective-permute-start.8
  46.9 1.8 slots.1
  48.7 1.6 collective-permute-done.8.refs_1_
  50.3 2.4 collective-permute-done.9.refs_2_
  52.7 5.3 %collective-permute-done.10.refs_3_ = bf16[128,768]{1,0:T(8,128)(2,1)S(1)} collective-permute-done((bf16[128,768]{1,0:T(8,128)(2,1)S(1)}, bf16[128,768]{1,0:T(8,128)(2,1)S(1)}, u32[]{:S(2)}, u32[]{:S(2)}) %collective-permute-start.10) | collective-permute-done | bytes 196640 | tf_op jit(solution)/shard_map/ppermute | solution.py:575
  58.6 3.2 collective-permute-start.12
  61.8 1.5 collective-permute-start.14
  64.0 1.4 collective-permute-done.11
  65.9 0.9 collective-permute-done.14.refs_1_.refs_0_
  66.9 4.3 %collective-permute-start.18 = (bf16[4,128,256]{2,1,0:T(8,128)(2,1)S(1)}, bf16[4,128,256]{2,1,0:T(8,128)(2,1)S(1)}, u32[]{:S(2)}, u32[]{:S(2)}) collective-permute-start(bf16[4,128,256]{2,1,0:T(8,128)(2,1)S(1)} %pad_maximum_fusion), channel_id=1, source_target_pairs={{4,0},{5,1},{6,2},{7,3},{8,4},{9,5},{10,6},{11,7},{12,8},{13,9},{1... | collective-permute-start | bytes 786440 | tf_op jit(solution)/shard_map/ppermute | solution.py:575
  71.2 1.3 collective-permute-start.16
  72.5 5.7 %collective-permute-done.16 = bf16[4,128,256]{2,1,0:T(8,128)(2,1)S(1)} collective-permute-done((bf16[4,128,256]{2,1,0:T(8,128)(2,1)S(1)}, bf16[4,128,256]{2,1,0:T(8,128)(2,1)S(1)}, u32[]{:S(2)}, u32[]{:S(2)}) %collective-permute-start.16) | collective-permute-done | bytes 262176 | tf_op jit(solution)/shard_map/ppermute | solution.py:575
  78.6 6.8 %collective-permute-start.20 = (bf16[2048,256]{1,0:T(8,128)(2,1)S(1)}, bf16[2048,256]{1,0:T(8,128)(2,1)S(1)}, u32[]{:S(2)}, u32[]{:S(2)}) collective-permute-start(bf16[2048,256]{1,0:T(8,128)(2,1)S(1)} %bitcast.36), channel_id=1, source_target_pairs={{1,0},{0,1},{3,2},{2,3},{5,4},{4,5},{7,6},{6,7},{9,8},{8,9},{11,10... | collective-permute-start | bytes 3145736 | tf_op jit(solution)/shard_map/ppermute | solution.py:575
  85.9 6.2 %attend.3.refs_3_.refs_5_ = f32[4,4,128,256]{3,2,1,0:T(8,128)S(1)} custom-call(bf16[128,512]{1,0:T(8,128)(2,1)S(1)} %get-tuple-element.80.refs_0_, bf16[128,512]{1,0:T(8,128)(2,1)S(1)} %collective-permute-done.14.refs_1_.refs_0_, bf16[128,512]{1,0:T(8,128)(2,1)S(1)} %collective-permute-done.19.refs_2_.refs_1_, ...), custom_call_target="tpu_custom_call" | custom-call | flops 8589934592 | bytes 8000000 | tf_op jit(solution)/shard_map/attend/pallas_call | solution.py:200
  92.1 4.6 %attend.5 = (bf16[128,640]{1,0:T(8,128)(2,1)S(1)}, bf16[128,640]{1,0:T(8,128)(2,1)S(1)}, bf16[128,640]{1,0:T(8,128)(2,1)S(1)}) custom-call(bf16[128,512]{1,0:T(8,128)(2,1)S(1)} %collective-permute-done.14.refs_1_.refs_0_, bf16[128,512]{1,0:T(8,128)(2,1)S(1)} %collective-permute-done.19.refs_2_.refs_1_, ...), custom_call_target="tpu_custom_call" | custom-call | flops 6442450944 | bytes 8000000 | tf_op jit(solution)/shard_map/attend/pallas_call | solution.py:200
  96.8 1.3 collective-permute-start.22
  98.3 1.5 attend.4.refs_0_
  100.4 2.2 collective-permute-done.21.refs_1_
  102.6 1.6 collective-permute-done.22.refs_2_
  104.2 3.8 collective-permute-done.23.refs_3_
  108.7 8.9 %finish.1 = (f32[128,4096]{1,0:T(8,128)}, bf16[128,4096]{1,0:T(8,128)(2,1)}, bf16[1024,3584]{1,0:T(8,128)(2,1)}) custom-call(bf16[128,640]{1,0:T(8,128)(2,1)} %copy-done, bf16[128,640]{1,0:T(8,128)(2,1)} %copy-done.4, bf16[128,640]{1,0:T(8,128)(2,1)} %copy-done.5, bf16[128,640]{1,0:T(8,128)(2,1)} %copy-done.6, ...), custom_call_target="tpu_custom_call" | custom-call | tf_op jit(solution)/shard_map/finish/pallas_call | solution.py:344
  117.6 8.9 %all-to-all-start.1 = ((bf16[128,8,3584]{2,1,0:T(8,128)(2,1)}), bf16[128,8,3584]{2,1,0:T(8,128)(2,1)}, u32[]{:S(2)}, u32[]{:S(2)}) async-start(bf16[128,8,3584]{2,1,0:T(8,128)(2,1)} %bitcast.43), calls=%async_computation.1 | async-start | bytes 14680064 | tf_op jit(solution)/shard_map/all_to_all | solution.py:673
  126.6 4.0 dispatch.1
  130.6 90.2 %all-to-all-done.1 = bf16[128,8,3584]{2,1,0:T(8,128)(2,1)} async-done(((bf16[128,8,3584]{2,1,0:T(8,128)(2,1)}), bf16[128,8,3584]{2,1,0:T(8,128)(2,1)}, u32[]{:S(2)}, u32[]{:S(2)}) %all-to-all-start.1) | async-done | bytes 7340064 | tf_op jit(solution)/shard_map/all_to_all | solution.py:673
  220.8 9.0 %all-to-all-start = ((bf16[128,8,1024]{2,1,0:T(8,128)(2,1)}), bf16[128,8,1024]{2,1,0:T(8,128)(2,1)S(1)}, u32[]{:S(2)}, u32[]{:S(2)}) async-start(bf16[128,8,1024]{2,1,0:T(8,128)(2,1)} %bitcast.42), calls=%async_computation | async-start | bytes 4194304 | tf_op jit(solution)/shard_map/all_to_all | solution.py:673
  229.8 22.0 %up_first.1 = (f32[1024,1536]{1,0:T(8,128)}, bf16[1024,512]{1,0:T(8,128)(2,1)}) custom-call(bf16[1024,3584]{1,0:T(8,128)(2,1)} %bitcast.17.x_ref, bf16[1,4096,1536]{2,1,0:T(8,128)(2,1)} %wu_ref.3, bf16[1,768,4096]{2,1,0:T(8,128)(2,1)} %wd_hbm.1), custom_call_target="tpu_custom_call" | custom-call | flops 9663676416 | bytes 20000000 | tf_op jit(solution)/shard_map/up_first/pallas_call | solution.py:423
  251.8 4.9 %all-to-all-done = bf16[128,8,1024]{2,1,0:T(8,128)(2,1)S(1)} async-done(((bf16[128,8,1024]{2,1,0:T(8,128)(2,1)}), bf16[128,8,1024]{2,1,0:T(8,128)(2,1)S(1)}, u32[]{:S(2)}, u32[]{:S(2)}) %all-to-all-start) | async-done | bytes 2097184 | tf_op jit(solution)/shard_map/all_to_all | solution.py:673
  256.7 1.3 copy-done.3
  258.0 17.6 %expert.1 = bf16[1024,4608]{1,0:T(8,128)(2,1)} custom-call(bf16[1024,1024]{1,0:T(8,128)(2,1)} %bitcast.41, bf16[1,4096,1536]{2,1,0:T(8,128)(2,1)} %wu_ref.3, f32[1024,1536]{1,0:T(8,128)} %get-tuple-element.98.partial_ref, bf16[1024,512]{1,0:T(8,128)(2,1)} %get-tuple-element.99.ninth_ref, bf16[1,768,4096]{2,1,0:T(8,128)(2,1)} %wd_hbm.1), custom_call_target="tpu_custom_call" | custom-call | flops 9663676416 | bytes 30000000 | tf_op jit(solution)/shard_map/expert/pallas_call | solution.py:473
  275.7 8.3 %all-to-all-start.2 = ((bf16[128,8,4608]{2,1,0:T(8,128)(2,1)}), bf16[128,8,4608]{2,1,0:T(8,128)(2,1)}, u32[]{:S(2)}, u32[]{:S(2)}) async-start(bf16[128,8,4608]{2,1,0:T(8,128)(2,1)} %bitcast.40), calls=%async_computation.2 | async-start | bytes 18874368 | tf_op jit(solution)/shard_map/all_to_all | solution.py:673
  283.9 3.2 weigh.1
  287.2 119.3 %all-to-all-done.2 = bf16[128,8,4608]{2,1,0:T(8,128)(2,1)} async-done(((bf16[128,8,4608]{2,1,0:T(8,128)(2,1)}), bf16[128,8,4608]{2,1,0:T(8,128)(2,1)}, u32[]{:S(2)}, u32[]{:S(2)}) %all-to-all-start.2) | async-done | bytes 9437216 | tf_op jit(solution)/shard_map/all_to_all | solution.py:673
  406.5 6.0 %combine.1 = bf16[128,4096]{1,0:T(8,128)(2,1)} custom-call(bf16[1024,4608]{1,0:T(8,128)(2,1)} %bitcast.19.x_ref.ninth_ref, bf16[1024,4608]{1,0:T(8,128)(2,1)} %bitcast.19.x_ref.ninth_ref, bf16[128,1024]{1,0:T(8,128)(2,1)} %get-tuple-element.102.w_ref, bf16[128,128]{1,0:T(8,128)(2,1)} %get-tuple-element.103.wlast_ref, f32[128,4096]{1,0:T(8,128)} %get-tuple-element.104.resid_ref), custom_call_target="tpu_custom_call" | custom-call | tf_op jit(solution)/shard_map/combine/pallas_call | solution.py:517
  (71 shorter events, 8.8 us)
Async XLA Ops:
  6.5 101.5 %all-gather.2.cloned.1.call-start = ((), (), s32[]{:S(2)}) async-start(), calls=%async_computation.3 | async-start | bytes 4456448 | tf_op jit(solution)/shard_map/all_gather | solution.py:630
  8.2 7.8 %collective-permute-start = (bf16[48,1024]{1,0:T(8,128)(2,1)S(1)}, bf16[48,1024]{1,0:T(8,128)(2,1)S(1)}, u32[]{:S(2)}, u32[]{:S(2)}) collective-permute-start(bf16[48,1024]{1,0:T(8,128)(2,1)S(1)} %dynamic-slice_bitcast_fusion.1), channel_id=1, source_target_pairs={{2,0},{3,1},{0,2},{1,3},{6,4},{7,5},{4,6},{5,7},{10,8},{11,9},{8,1... | collective-permute-start | bytes 294920 | tf_op jit(solution)/shard_map/ppermute | solution.py:575
  15.9 42.1 %copy-start.1 = (bf16[128]{0:T(256)(128)(2,1)S(1)}, bf16[128]{0:T(256)(128)(2,1)}, u32[]{:S(2)}) copy-start(bf16[128]{0:T(256)(128)(2,1)} %param.15) | copy-start | bytes 772
  15.9 42.1 %copy-start.2 = (bf16[128]{0:T(256)(128)(2,1)S(1)}, bf16[128]{0:T(256)(128)(2,1)}, u32[]{:S(2)}) copy-start(bf16[128]{0:T(256)(128)(2,1)} %param.16) | copy-start | bytes 772
  16.0 15.9 %collective-permute-start.3 = (bf16[2,48,1024]{2,1,0:T(8,128)(2,1)S(1)}, bf16[2,48,1024]{2,1,0:T(8,128)(2,1)S(1)}, u32[]{:S(2)}, u32[]{:S(2)}) collective-permute-start(bf16[2,48,1024]{2,1,0:T(8,128)(2,1)S(1)} %pad_maximum_fusion.1), channel_id=1, source_target_pairs={{4,0},{5,1},{6,2},{7,3},{8,4},{9,5},{10,6},{11,7},{12,8},{13,9},{1... | collective-permute-start | bytes 589832 | tf_op jit(solution)/shard_map/ppermute | solution.py:575
  16.2 15.6 %collective-permute-start.2 = (bf16[2,48,1024]{2,1,0:T(8,128)(2,1)S(1)}, bf16[2,48,1024]{2,1,0:T(8,128)(2,1)S(1)}, u32[]{:S(2)}, u32[]{:S(2)}) collective-permute-start(bf16[2,48,1024]{2,1,0:T(8,128)(2,1)S(1)} %pad_maximum_fusion.1), channel_id=1, source_target_pairs={{8,0},{9,1},{10,2},{11,3},{12,4},{13,5},{14,6},{15,7},{0,8},{1,9},... | collective-permute-start | bytes 589832 | tf_op jit(solution)/shard_map/ppermute | solution.py:575
  18.5 12.1 %collective-permute-start.1 = (bf16[2,48,1024]{2,1,0:T(8,128)(2,1)S(1)}, bf16[2,48,1024]{2,1,0:T(8,128)(2,1)S(1)}, u32[]{:S(2)}, u32[]{:S(2)}) collective-permute-start(bf16[2,48,1024]{2,1,0:T(8,128)(2,1)S(1)} %pad_maximum_fusion.1), channel_id=1, source_target_pairs={{12,0},{13,1},{14,2},{15,3},{0,4},{1,5},{2,6},{3,7},{4,8},{5,9},{6... | collective-permute-start | bytes 589832 | tf_op jit(solution)/shard_map/ppermute | solution.py:575
  20.2 11.7 %collective-permute-start.6 = (bf16[128,1024]{1,0:T(8,128)(2,1)S(1)}, bf16[128,1024]{1,0:T(8,128)(2,1)S(1)}, u32[]{:S(2)}, u32[]{:S(2)}) collective-permute-start(bf16[128,1024]{1,0:T(8,128)(2,1)S(1)} %get-tuple-element.109), channel_id=1, source_target_pairs={{16,0},{17,1},{18,2},{19,3},{20,4},{21,5},{22,6},{23,7},{24,8},{25... | collective-permute-start | bytes 786440 | tf_op jit(solution)/shard_map/ppermute | solution.py:575
  22.8 9.1 %collective-permute-start.5 = (bf16[128,1024]{1,0:T(8,128)(2,1)S(1)}, bf16[128,1024]{1,0:T(8,128)(2,1)S(1)}, u32[]{:S(2)}, u32[]{:S(2)}) collective-permute-start(bf16[128,1024]{1,0:T(8,128)(2,1)S(1)} %get-tuple-element.110), channel_id=1, source_target_pairs={{32,0},{33,1},{34,2},{35,3},{36,4},{37,5},{38,6},{39,7},{40,8},{41... | collective-permute-start | bytes 786440 | tf_op jit(solution)/shard_map/ppermute | solution.py:575
  30.6 7.9 %collective-permute-start.4 = (bf16[128,1024]{1,0:T(8,128)(2,1)S(1)}, bf16[128,1024]{1,0:T(8,128)(2,1)S(1)}, u32[]{:S(2)}, u32[]{:S(2)}) collective-permute-start(bf16[128,1024]{1,0:T(8,128)(2,1)S(1)} %get-tuple-element.111), channel_id=1, source_target_pairs={{48,0},{49,1},{50,2},{51,3},{52,4},{53,5},{54,6},{55,7},{56,8},{57... | collective-permute-start | bytes 786440 | tf_op jit(solution)/shard_map/ppermute | solution.py:575
  31.9 53.5 %copy-start.7 = (bf16[4096]{0:T(1024)(128)(2,1)S(1)}, bf16[4096]{0:T(1024)(128)(2,1)}, u32[]{:S(2)}) copy-start(bf16[4096]{0:T(1024)(128)(2,1)} %param.19) | copy-start | bytes 24580
  38.5 3.9 collective-permute-start.7
  44.0 6.3 %collective-permute-start.8 = (bf16[128,768]{1,0:T(8,128)(2,1)S(1)}, bf16[128,768]{1,0:T(8,128)(2,1)S(1)}, u32[]{:S(2)}, u32[]{:S(2)}) collective-permute-start(bf16[128,768]{1,0:T(8,128)(2,1)S(1)} %get-tuple-element.67), channel_id=1, source_target_pairs={{16,0},{17,1},{18,2},{19,3},{20,4},{21,5},{22,6},{23,7},{24,8},{25... | collective-permute-start | bytes 589832 | tf_op jit(solution)/shard_map/ppermute | solution.py:575
  45.4 7.3 %collective-permute-start.9 = (bf16[128,768]{1,0:T(8,128)(2,1)S(1)}, bf16[128,768]{1,0:T(8,128)(2,1)S(1)}, u32[]{:S(2)}, u32[]{:S(2)}) collective-permute-start(bf16[128,768]{1,0:T(8,128)(2,1)S(1)} %get-tuple-element.68), channel_id=1, source_target_pairs={{32,0},{33,1},{34,2},{35,3},{36,4},{37,5},{38,6},{39,7},{40,8},{41... | collective-permute-start | bytes 589832 | tf_op jit(solution)/shard_map/ppermute | solution.py:575
  45.9 12.1 %collective-permute-start.10 = (bf16[128,768]{1,0:T(8,128)(2,1)S(1)}, bf16[128,768]{1,0:T(8,128)(2,1)S(1)}, u32[]{:S(2)}, u32[]{:S(2)}) collective-permute-start(bf16[128,768]{1,0:T(8,128)(2,1)S(1)} %get-tuple-element.69), channel_id=1, source_target_pairs={{48,0},{49,1},{50,2},{51,3},{52,4},{53,5},{54,6},{55,7},{56,8},{57... | collective-permute-start | bytes 589832 | tf_op jit(solution)/shard_map/ppermute | solution.py:575
  58.5 4.8 %collective-permute-start.13 = (bf16[128,256]{1,0:T(8,128)(2,1)S(1)}, bf16[128,256]{1,0:T(8,128)(2,1)S(1)}, u32[]{:S(2)}, u32[]{:S(2)}) collective-permute-start(bf16[128,256]{1,0:T(8,128)(2,1)S(1)} %get-tuple-element.81), channel_id=1, source_target_pairs={{66,0},{67,1},{64,2},{65,3},{70,4},{71,5},{68,6},{69,7},{74,8},{75... | collective-permute-start | bytes 196616 | tf_op jit(solution)/shard_map/ppermute | solution.py:575
  58.6 5.4 %collective-permute-start.12 = (bf16[128,256]{1,0:T(8,128)(2,1)S(1)}, bf16[128,256]{1,0:T(8,128)(2,1)S(1)}, u32[]{:S(2)}, u32[]{:S(2)}) collective-permute-start(bf16[128,256]{1,0:T(8,128)(2,1)S(1)} %get-tuple-element.81), channel_id=1, source_target_pairs={{2,0},{3,1},{0,2},{1,3},{6,4},{7,5},{4,6},{5,7},{10,8},{11,9},{8,1... | collective-permute-start | bytes 196616 | tf_op jit(solution)/shard_map/ppermute | solution.py:575
  61.8 3.6 collective-permute-start.11
  61.8 4.1 collective-permute-start.15
  61.8 5.0 %collective-permute-start.14 = (bf16[128,512]{1,0:T(8,128)(2,1)S(1)}, bf16[128,512]{1,0:T(8,128)(2,1)S(1)}, u32[]{:S(2)}, u32[]{:S(2)}) collective-permute-start(bf16[128,512]{1,0:T(8,128)(2,1)S(1)} %get-tuple-element.80.refs_0_), channel_id=1, source_target_pairs={{48,0},{49,1},{50,2},{51,3},{52,4},{53,5},{54,6},{55,7},{56,8},{57... | collective-permute-start | bytes 393224 | tf_op jit(solution)/shard_map/ppermute | solution.py:575
  63.3 15.3 %collective-permute-start.19 = (bf16[128,512]{1,0:T(8,128)(2,1)S(1)}, bf16[128,512]{1,0:T(8,128)(2,1)S(1)}, u32[]{:S(2)}, u32[]{:S(2)}) collective-permute-start(bf16[128,512]{1,0:T(8,128)(2,1)S(1)} %get-tuple-element.80.refs_0_), channel_id=1, source_target_pairs={{32,0},{33,1},{34,2},{35,3},{36,4},{37,5},{38,6},{39,7},{40,8},{41... | collective-permute-start | bytes 393224 | tf_op jit(solution)/shard_map/ppermute | solution.py:575
  66.9 11.6 %collective-permute-start.18 = (bf16[4,128,256]{2,1,0:T(8,128)(2,1)S(1)}, bf16[4,128,256]{2,1,0:T(8,128)(2,1)S(1)}, u32[]{:S(2)}, u32[]{:S(2)}) collective-permute-start(bf16[4,128,256]{2,1,0:T(8,128)(2,1)S(1)} %pad_maximum_fusion), channel_id=1, source_target_pairs={{4,0},{5,1},{6,2},{7,3},{8,4},{9,5},{10,6},{11,7},{12,8},{13,9},{1... | collective-permute-start | bytes 786440 | tf_op jit(solution)/shard_map/ppermute | solution.py:575
  71.2 7.3 %collective-permute-start.17 = (bf16[4,128,256]{2,1,0:T(8,128)(2,1)S(1)}, bf16[4,128,256]{2,1,0:T(8,128)(2,1)S(1)}, u32[]{:S(2)}, u32[]{:S(2)}) collective-permute-start(bf16[4,128,256]{2,1,0:T(8,128)(2,1)S(1)} %pad_maximum_fusion), channel_id=1, source_target_pairs={{8,0},{9,1},{10,2},{11,3},{12,4},{13,5},{14,6},{15,7},{0,8},{1,9},... | collective-permute-start | bytes 786440 | tf_op jit(solution)/shard_map/ppermute | solution.py:575
  71.2 7.0 %collective-permute-start.16 = (bf16[4,128,256]{2,1,0:T(8,128)(2,1)S(1)}, bf16[4,128,256]{2,1,0:T(8,128)(2,1)S(1)}, u32[]{:S(2)}, u32[]{:S(2)}) collective-permute-start(bf16[4,128,256]{2,1,0:T(8,128)(2,1)S(1)} %pad_maximum_fusion), channel_id=1, source_target_pairs={{12,0},{13,1},{14,2},{15,3},{0,4},{1,5},{2,6},{3,7},{4,8},{5,9},{6... | collective-permute-start | bytes 786440 | tf_op jit(solution)/shard_map/ppermute | solution.py:575
  78.6 13.5 %collective-permute-start.20 = (bf16[2048,256]{1,0:T(8,128)(2,1)S(1)}, bf16[2048,256]{1,0:T(8,128)(2,1)S(1)}, u32[]{:S(2)}, u32[]{:S(2)}) collective-permute-start(bf16[2048,256]{1,0:T(8,128)(2,1)S(1)} %bitcast.36), channel_id=1, source_target_pairs={{1,0},{0,1},{3,2},{2,3},{5,4},{4,5},{7,6},{6,7},{9,8},{8,9},{11,10... | collective-permute-start | bytes 3145736 | tf_op jit(solution)/shard_map/ppermute | solution.py:575
  96.7 5.9 %collective-permute-start.21 = (bf16[128,640]{1,0:T(8,128)(2,1)S(1)}, bf16[128,640]{1,0:T(8,128)(2,1)S(1)}, u32[]{:S(2)}, u32[]{:S(2)}) collective-permute-start(bf16[128,640]{1,0:T(8,128)(2,1)S(1)} %get-tuple-element.90), channel_id=1, source_target_pairs={{16,0},{17,1},{18,2},{19,3},{20,4},{21,5},{22,6},{23,7},{24,8},{25... | collective-permute-start | bytes 491528 | tf_op jit(solution)/shard_map/ppermute | solution.py:575
  96.8 7.4 %collective-permute-start.22 = (bf16[128,640]{1,0:T(8,128)(2,1)S(1)}, bf16[128,640]{1,0:T(8,128)(2,1)S(1)}, u32[]{:S(2)}, u32[]{:S(2)}) collective-permute-start(bf16[128,640]{1,0:T(8,128)(2,1)S(1)} %get-tuple-element.91), channel_id=1, source_target_pairs={{32,0},{33,1},{34,2},{35,3},{36,4},{37,5},{38,6},{39,7},{40,8},{41... | collective-permute-start | bytes 491528 | tf_op jit(solution)/shard_map/ppermute | solution.py:575
  98.1 9.9 %collective-permute-start.23 = (bf16[128,640]{1,0:T(8,128)(2,1)S(1)}, bf16[128,640]{1,0:T(8,128)(2,1)S(1)}, u32[]{:S(2)}, u32[]{:S(2)}) collective-permute-start(bf16[128,640]{1,0:T(8,128)(2,1)S(1)} %get-tuple-element.92), channel_id=1, source_target_pairs={{48,0},{49,1},{50,2},{51,3},{52,4},{53,5},{54,6},{55,7},{56,8},{57... | collective-permute-start | bytes 491528 | tf_op jit(solution)/shard_map/ppermute | solution.py:575
  99.8 0.7 copy-start
  102.6 5.4 %copy-start.4 = (bf16[128,640]{1,0:T(8,128)(2,1)}, bf16[128,640]{1,0:T(8,128)(2,1)S(1)}, u32[]{:S(2)}) copy-start(bf16[128,640]{1,0:T(8,128)(2,1)S(1)} %collective-permute-done.21.refs_1_) | copy-start | bytes 491524
  104.2 3.8 copy-start.5
  108.0 0.7 copy-start.6
  117.6 103.2 %all-to-all-start.1 = ((bf16[128,8,3584]{2,1,0:T(8,128)(2,1)}), bf16[128,8,3584]{2,1,0:T(8,128)(2,1)}, u32[]{:S(2)}, u32[]{:S(2)}) async-start(bf16[128,8,3584]{2,1,0:T(8,128)(2,1)} %bitcast.43), calls=%async_computation.1 | async-start | bytes 14680064 | tf_op jit(solution)/shard_map/all_to_all | solution.py:673
  220.8 35.9 %all-to-all-start = ((bf16[128,8,1024]{2,1,0:T(8,128)(2,1)}), bf16[128,8,1024]{2,1,0:T(8,128)(2,1)S(1)}, u32[]{:S(2)}, u32[]{:S(2)}) async-start(bf16[128,8,1024]{2,1,0:T(8,128)(2,1)} %bitcast.42), calls=%async_computation | async-start | bytes 4194304 | tf_op jit(solution)/shard_map/all_to_all | solution.py:673
  256.7 1.3 copy-start.3
  275.7 130.8 %all-to-all-start.2 = ((bf16[128,8,4608]{2,1,0:T(8,128)(2,1)}), bf16[128,8,4608]{2,1,0:T(8,128)(2,1)}, u32[]{:S(2)}, u32[]{:S(2)}) async-start(bf16[128,8,4608]{2,1,0:T(8,128)(2,1)} %bitcast.40), calls=%async_computation.2 | async-start | bytes 18874368 | tf_op jit(solution)/shard_map/all_to_all | solution.py:673
Sparse Core Ops, SparseCore 0:
  9.8 59.0 all-gather.1
where the time goes:
time: 423 us; the launch traced here: 419 us
  waiting for transfers between devices  256 us (61%)
  Pallas kernels  78 us (18%)
  starting transfers between devices  61.1 us (14%)
  between operations  13.8 us (3%)
  local copies, waits for them, and re-layouts  5.6 us (1%)
  other arithmetic  4.6 us (1%)
    all_to_all x3, waiting for transfers between devices, exchange(): lax.all_to_all(x.reshape(count, GROUP, wide), ('ctx', 'exp'), split_axis=...  214 us
    ppermute x24, waiting for transfers between devices, bring(): return lax.ppermute(value, ('ctx', 'exp'), pairs)  41.1 us
    ppermute x24, starting transfers between devices, bring(): return lax.ppermute(value, ('ctx', 'exp'), pairs)  34.9 us
    all_to_all x3, starting transfers between devices, exchange(): lax.all_to_all(x.reshape(count, GROUP, wide), ('ctx', 'exp'), split_axis=...  26.2 us
    pallas_call x1, Pallas kernels, up_first(): pl.pallas_call(functools.partial(up_kernel, features), grid=(blocks,), in...  22 us
    pallas_call x1, Pallas kernels, expert(): pl.pallas_call(expert_kernel, grid=(blocks,), in_specs=[pl.BlockSpec((row...  17.6 us
    pallas_call x3, Pallas kernels, attend(): pl.pallas_call(functools.partial(attend_kernel, heads, size, 512, ring, l...  12.3 us
    pallas_call x1, Pallas kernels, finish(): pl.pallas_call(functools.partial(finish_kernel, heads, size, features), g...  8.95 us
  transfers between devices with their start and end apart: 28, of which 17 were waited for; matrix products, arithmetic and copies ran while one was open for 2% of the time, Pallas kernels for 11%

commit v1 on v0

--- a/solution.py
+++ b/solution.py
@@ -340,7 +340,7 @@
 def finish(parts, w_out, tokens, gain, pick, last, heads, size, features):
     rows, count = pick.shape[0], last.shape[0]
     wide = features + tokens.shape[1] // GROUP
-    blocks = 4
+    blocks = 2
     return pl.pallas_call(
         functools.partial(finish_kernel, heads, size, features),
         grid=(blocks,),

time: 423 us -> 422 us (level)
  no operation moved by 1% of the time
where the time goes in v1:
time: 422 us; the launch traced here: 419 us
  waiting for transfers between devices  256 us (61%)
  Pallas kernels  77.5 us (18%)
  starting transfers between devices  61.1 us (14%)
  between operations  13.8 us (3%)
  local copies, waits for them, and re-layouts  5.6 us (1%)
  other arithmetic  4.6 us (1%)
    all_to_all x3, waiting for transfers between devices, exchange(): lax.all_to_all(x.reshape(count, GROUP, wide), ('ctx', 'exp'), split_axis=...  214 us
    ppermute x24, waiting for transfers between devices, bring(): return lax.ppermute(value, ('ctx', 'exp'), pairs)  41.1 us
    ppermute x24, starting transfers between devices, bring(): return lax.ppermute(value, ('ctx', 'exp'), pairs)  34.9 us
    all_to_all x3, starting transfers between devices, exchange(): lax.all_to_all(x.reshape(count, GROUP, wide), ('ctx', 'exp'), split_axis=...  26.2 us
    pallas_call x1, Pallas kernels, up_first(): pl.pallas_call(functools.partial(up_kernel, features), grid=(blocks,), in...  22 us
    pallas_call x1, Pallas kernels, expert(): pl.pallas_call(expert_kernel, grid=(blocks,), in_specs=[pl.BlockSpec((row...  17.6 us
    pallas_call x3, Pallas kernels, attend(): pl.pallas_call(functools.partial(attend_kernel, heads, size, 512, ring, l...  12.3 us
  transfers between devices with their start and end apart: 28, of which 17 were waited for; matrix products, arithmetic and copies ran while one was open for 2% of the time, Pallas kernels for 11%

profile of v1, /device:TPU:41, one launch (start us, length us, event | category | flops | bytes accessed | tf_op | source)
XLA Modules:
  0.0 418.8 jit_solution(14662213867915487791)
XLA Ops:
  7.3 0.9 dynamic-slice_bitcast_fusion.1
  8.2 2.7 collective-permute-start
  11.6 0.8 select_reduce_fusion.1
  12.5 0.8 select_reduce_fusion
  13.4 0.9 constant_dynamic-update-slice_fusion.4
  14.3 1.6 fusion.1
  16.2 2.3 collective-permute-start.2
  18.5 1.6 collective-permute-start.1
  20.2 2.5 collective-permute-start.6
  23.3 7.3 %collective-permute-done.1 = bf16[2,48,1024]{2,1,0:T(8,128)(2,1)S(1)} collective-permute-done((bf16[2,48,1024]{2,1,0:T(8,128)(2,1)S(1)}, bf16[2,48,1024]{2,1,0:T(8,128)(2,1)S(1)}, u32[]{:S(2)}, u32[]{:S(2)}) %collective-permute-start.1) | collective-permute-done | bytes 196640 | tf_op jit(solution)/shard_map/ppermute | solution.py:575
  30.6 1.2 collective-permute-start.4
  31.9 6.6 %collective-permute-done.4.refs_1_ = bf16[128,1024]{1,0:T(8,128)(2,1)S(1)} collective-permute-done((bf16[128,1024]{1,0:T(8,128)(2,1)S(1)}, bf16[128,1024]{1,0:T(8,128)(2,1)S(1)}, u32[]{:S(2)}, u32[]{:S(2)}) %collective-permute-start.4) | collective-permute-done | bytes 262176 | tf_op jit(solution)/shard_map/ppermute | solution.py:575
  38.5 2.0 collective-permute-start.7
  41.0 1.4 collective-permute-done.7.refs_5_
  42.4 1.6 project.1
  44.0 1.4 collective-permute-start.8
  46.9 1.8 slots.1
  48.7 1.6 collective-permute-done.8.refs_1_
  50.3 2.4 collective-permute-done.9.refs_2_
  52.7 5.3 %collective-permute-done.10.refs_3_ = bf16[128,768]{1,0:T(8,128)(2,1)S(1)} collective-permute-done((bf16[128,768]{1,0:T(8,128)(2,1)S(1)}, bf16[128,768]{1,0:T(8,128)(2,1)S(1)}, u32[]{:S(2)}, u32[]{:S(2)}) %collective-permute-start.10) | collective-permute-done | bytes 196640 | tf_op jit(solution)/shard_map/ppermute | solution.py:575
  58.6 3.2 collective-permute-start.12
  61.8 1.5 collective-permute-start.14
  64.0 1.4 collective-permute-done.11
  65.9 0.9 collective-permute-done.14.refs_1_.refs_0_
  66.9 4.3 %collective-permute-start.18 = (bf16[4,128,256]{2,1,0:T(8,128)(2,1)S(1)}, bf16[4,128,256]{2,1,0:T(8,128)(2,1)S(1)}, u32[]{:S(2)}, u32[]{:S(2)}) collective-permute-start(bf16[4,128,256]{2,1,0:T(8,128)(2,1)S(1)} %pad_maximum_fusion), channel_id=1, source_target_pairs={{4,0},{5,1},{6,2},{7,3},{8,4},{9,5},{10,6},{11,7},{12,8},{13,9},{1... | collective-permute-start | bytes 786440 | tf_op jit(solution)/shard_map/ppermute | solution.py:575
  71.2 1.3 collective-permute-start.16
  72.5 5.7 %collective-permute-done.16 = bf16[4,128,256]{2,1,0:T(8,128)(2,1)S(1)} collective-permute-done((bf16[4,128,256]{2,1,0:T(8,128)(2,1)S(1)}, bf16[4,128,256]{2,1,0:T(8,128)(2,1)S(1)}, u32[]{:S(2)}, u32[]{:S(2)}) %collective-permute-start.16) | collective-permute-done | bytes 262176 | tf_op jit(solution)/shard_map/ppermute | solution.py:575
  78.6 6.8 %collective-permute-start.20 = (bf16[2048,256]{1,0:T(8,128)(2,1)S(1)}, bf16[2048,256]{1,0:T(8,128)(2,1)S(1)}, u32[]{:S(2)}, u32[]{:S(2)}) collective-permute-start(bf16[2048,256]{1,0:T(8,128)(2,1)S(1)} %bitcast.36), channel_id=1, source_target_pairs={{1,0},{0,1},{3,2},{2,3},{5,4},{4,5},{7,6},{6,7},{9,8},{8,9},{11,10... | collective-permute-start | bytes 3145736 | tf_op jit(solution)/shard_map/ppermute | solution.py:575
  85.9 6.2 %attend.3.refs_3_.refs_5_ = f32[4,4,128,256]{3,2,1,0:T(8,128)S(1)} custom-call(bf16[128,512]{1,0:T(8,128)(2,1)S(1)} %get-tuple-element.80.refs_0_, bf16[128,512]{1,0:T(8,128)(2,1)S(1)} %collective-permute-done.14.refs_1_.refs_0_, bf16[128,512]{1,0:T(8,128)(2,1)S(1)} %collective-permute-done.19.refs_2_.refs_1_, ...), custom_call_target="tpu_custom_call" | custom-call | flops 8589934592 | bytes 8000000 | tf_op jit(solution)/shard_map/attend/pallas_call | solution.py:200
  92.1 4.6 %attend.5 = (bf16[128,640]{1,0:T(8,128)(2,1)S(1)}, bf16[128,640]{1,0:T(8,128)(2,1)S(1)}, bf16[128,640]{1,0:T(8,128)(2,1)S(1)}) custom-call(bf16[128,512]{1,0:T(8,128)(2,1)S(1)} %collective-permute-done.14.refs_1_.refs_0_, bf16[128,512]{1,0:T(8,128)(2,1)S(1)} %collective-permute-done.19.refs_2_.refs_1_, ...), custom_call_target="tpu_custom_call" | custom-call | flops 6442450944 | bytes 8000000 | tf_op jit(solution)/shard_map/attend/pallas_call | solution.py:200
  96.8 1.3 collective-permute-start.22
  98.3 1.5 attend.4.refs_0_
  100.4 2.2 collective-permute-done.21.refs_1_
  102.6 1.6 collective-permute-done.22.refs_2_
  104.2 3.8 collective-permute-done.23.refs_3_
  108.7 8.4 %finish.1 = (f32[128,4096]{1,0:T(8,128)}, bf16[128,4096]{1,0:T(8,128)(2,1)}, bf16[1024,3584]{1,0:T(8,128)(2,1)}) custom-call(bf16[128,640]{1,0:T(8,128)(2,1)} %copy-done, bf16[128,640]{1,0:T(8,128)(2,1)} %copy-done.4, bf16[128,640]{1,0:T(8,128)(2,1)} %copy-done.5, bf16[128,640]{1,0:T(8,128)(2,1)} %copy-done.6, ...), custom_call_target="tpu_custom_call" | custom-call | tf_op jit(solution)/shard_map/finish/pallas_call | solution.py:344
  117.1 8.9 %all-to-all-start.1 = ((bf16[128,8,3584]{2,1,0:T(8,128)(2,1)}), bf16[128,8,3584]{2,1,0:T(8,128)(2,1)}, u32[]{:S(2)}, u32[]{:S(2)}) async-start(bf16[128,8,3584]{2,1,0:T(8,128)(2,1)} %bitcast.43), calls=%async_computation.1 | async-start | bytes 14680064 | tf_op jit(solution)/shard_map/all_to_all | solution.py:673
  126.0 4.0 dispatch.1
  130.0 90.2 %all-to-all-done.1 = bf16[128,8,3584]{2,1,0:T(8,128)(2,1)} async-done(((bf16[128,8,3584]{2,1,0:T(8,128)(2,1)}), bf16[128,8,3584]{2,1,0:T(8,128)(2,1)}, u32[]{:S(2)}, u32[]{:S(2)}) %all-to-all-start.1) | async-done | bytes 7340064 | tf_op jit(solution)/shard_map/all_to_all | solution.py:673
  220.2 9.0 %all-to-all-start = ((bf16[128,8,1024]{2,1,0:T(8,128)(2,1)}), bf16[128,8,1024]{2,1,0:T(8,128)(2,1)S(1)}, u32[]{:S(2)}, u32[]{:S(2)}) async-start(bf16[128,8,1024]{2,1,0:T(8,128)(2,1)} %bitcast.42), calls=%async_computation | async-start | bytes 4194304 | tf_op jit(solution)/shard_map/all_to_all | solution.py:673
  229.2 22.0 %up_first.1 = (f32[1024,1536]{1,0:T(8,128)}, bf16[1024,512]{1,0:T(8,128)(2,1)}) custom-call(bf16[1024,3584]{1,0:T(8,128)(2,1)} %bitcast.17.x_ref, bf16[1,4096,1536]{2,1,0:T(8,128)(2,1)} %wu_ref.3, bf16[1,768,4096]{2,1,0:T(8,128)(2,1)} %wd_hbm.1), custom_call_target="tpu_custom_call" | custom-call | flops 9663676416 | bytes 20000000 | tf_op jit(solution)/shard_map/up_first/pallas_call | solution.py:423
  251.3 4.9 %all-to-all-done = bf16[128,8,1024]{2,1,0:T(8,128)(2,1)S(1)} async-done(((bf16[128,8,1024]{2,1,0:T(8,128)(2,1)}), bf16[128,8,1024]{2,1,0:T(8,128)(2,1)S(1)}, u32[]{:S(2)}, u32[]{:S(2)}) %all-to-all-start) | async-done | bytes 2097184 | tf_op jit(solution)/shard_map/all_to_all | solution.py:673
  256.1 1.3 copy-done.3
  257.4 17.6 %expert.1 = bf16[1024,4608]{1,0:T(8,128)(2,1)} custom-call(bf16[1024,1024]{1,0:T(8,128)(2,1)} %bitcast.41, bf16[1,4096,1536]{2,1,0:T(8,128)(2,1)} %wu_ref.3, f32[1024,1536]{1,0:T(8,128)} %get-tuple-element.98.partial_ref, bf16[1024,512]{1,0:T(8,128)(2,1)} %get-tuple-element.99.ninth_ref, bf16[1,768,4096]{2,1,0:T(8,128)(2,1)} %wd_hbm.1), custom_call_target="tpu_custom_call" | custom-call | flops 9663676416 | bytes 30000000 | tf_op jit(solution)/shard_map/expert/pallas_call | solution.py:473
  275.1 8.3 %all-to-all-start.2 = ((bf16[128,8,4608]{2,1,0:T(8,128)(2,1)}), bf16[128,8,4608]{2,1,0:T(8,128)(2,1)}, u32[]{:S(2)}, u32[]{:S(2)}) async-start(bf16[128,8,4608]{2,1,0:T(8,128)(2,1)} %bitcast.40), calls=%async_computation.2 | async-start | bytes 18874368 | tf_op jit(solution)/shard_map/all_to_all | solution.py:673
  283.4 3.2 weigh.1
  286.6 119.3 %all-to-all-done.2 = bf16[128,8,4608]{2,1,0:T(8,128)(2,1)} async-done(((bf16[128,8,4608]{2,1,0:T(8,128)(2,1)}), bf16[128,8,4608]{2,1,0:T(8,128)(2,1)}, u32[]{:S(2)}, u32[]{:S(2)}) %all-to-all-start.2) | async-done | bytes 9437216 | tf_op jit(solution)/shard_map/all_to_all | solution.py:673
  405.9 6.0 %combine.1 = bf16[128,4096]{1,0:T(8,128)(2,1)} custom-call(bf16[1024,4608]{1,0:T(8,128)(2,1)} %bitcast.19.x_ref.ninth_ref, bf16[1024,4608]{1,0:T(8,128)(2,1)} %bitcast.19.x_ref.ninth_ref, bf16[128,1024]{1,0:T(8,128)(2,1)} %get-tuple-element.102.w_ref, bf16[128,128]{1,0:T(8,128)(2,1)} %get-tuple-element.103.wlast_ref, f32[128,4096]{1,0:T(8,128)} %get-tuple-element.104.resid_ref), custom_call_target="tpu_custom_call" | custom-call | tf_op jit(solution)/shard_map/combine/pallas_call | solution.py:517
  (71 shorter events, 8.8 us)
Async XLA Ops:
  6.5 101.5 %all-gather.2.cloned.1.call-start = ((), (), s32[]{:S(2)}) async-start(), calls=%async_computation.3 | async-start | bytes 4456448 | tf_op jit(solution)/shard_map/all_gather | solution.py:630
  8.2 7.8 %collective-permute-start = (bf16[48,1024]{1,0:T(8,128)(2,1)S(1)}, bf16[48,1024]{1,0:T(8,128)(2,1)S(1)}, u32[]{:S(2)}, u32[]{:S(2)}) collective-permute-start(bf16[48,1024]{1,0:T(8,128)(2,1)S(1)} %dynamic-slice_bitcast_fusion.1), channel_id=1, source_target_pairs={{2,0},{3,1},{0,2},{1,3},{6,4},{7,5},{4,6},{5,7},{10,8},{11,9},{8,1... | collective-permute-start | bytes 294920 | tf_op jit(solution)/shard_map/ppermute | solution.py:575
  15.9 42.1 %copy-start.1 = (bf16[128]{0:T(256)(128)(2,1)S(1)}, bf16[128]{0:T(256)(128)(2,1)}, u32[]{:S(2)}) copy-start(bf16[128]{0:T(256)(128)(2,1)} %param.15) | copy-start | bytes 772
  15.9 42.1 %copy-start.2 = (bf16[128]{0:T(256)(128)(2,1)S(1)}, bf16[128]{0:T(256)(128)(2,1)}, u32[]{:S(2)}) copy-start(bf16[128]{0:T(256)(128)(2,1)} %param.16) | copy-start | bytes 772
  16.0 15.9 %collective-permute-start.3 = (bf16[2,48,1024]{2,1,0:T(8,128)(2,1)S(1)}, bf16[2,48,1024]{2,1,0:T(8,128)(2,1)S(1)}, u32[]{:S(2)}, u32[]{:S(2)}) collective-permute-start(bf16[2,48,1024]{2,1,0:T(8,128)(2,1)S(1)} %pad_maximum_fusion.1), channel_id=1, source_target_pairs={{4,0},{5,1},{6,2},{7,3},{8,4},{9,5},{10,6},{11,7},{12,8},{13,9},{1... | collective-permute-start | bytes 589832 | tf_op jit(solution)/shard_map/ppermute | solution.py:575
  16.2 15.6 %collective-permute-start.2 = (bf16[2,48,1024]{2,1,0:T(8,128)(2,1)S(1)}, bf16[2,48,1024]{2,1,0:T(8,128)(2,1)S(1)}, u32[]{:S(2)}, u32[]{:S(2)}) collective-permute-start(bf16[2,48,1024]{2,1,0:T(8,128)(2,1)S(1)} %pad_maximum_fusion.1), channel_id=1, source_target_pairs={{8,0},{9,1},{10,2},{11,3},{12,4},{13,5},{14,6},{15,7},{0,8},{1,9},... | collective-permute-start | bytes 589832 | tf_op jit(solution)/shard_map/ppermute | solution.py:575
  18.5 12.1 %collective-permute-start.1 = (bf16[2,48,1024]{2,1,0:T(8,128)(2,1)S(1)}, bf16[2,48,1024]{2,1,0:T(8,128)(2,1)S(1)}, u32[]{:S(2)}, u32[]{:S(2)}) collective-permute-start(bf16[2,48,1024]{2,1,0:T(8,128)(2,1)S(1)} %pad_maximum_fusion.1), channel_id=1, source_target_pairs={{12,0},{13,1},{14,2},{15,3},{0,4},{1,5},{2,6},{3,7},{4,8},{5,9},{6... | collective-permute-start | bytes 589832 | tf_op jit(solution)/shard_map/ppermute | solution.py:575
  20.2 11.7 %collective-permute-start.6 = (bf16[128,1024]{1,0:T(8,128)(2,1)S(1)}, bf16[128,1024]{1,0:T(8,128)(2,1)S(1)}, u32[]{:S(2)}, u32[]{:S(2)}) collective-permute-start(bf16[128,1024]{1,0:T(8,128)(2,1)S(1)} %get-tuple-element.109), channel_id=1, source_target_pairs={{16,0},{17,1},{18,2},{19,3},{20,4},{21,5},{22,6},{23,7},{24,8},{25... | collective-permute-start | bytes 786440 | tf_op jit(solution)/shard_map/ppermute | solution.py:575
  22.8 9.1 %collective-permute-start.5 = (bf16[128,1024]{1,0:T(8,128)(2,1)S(1)}, bf16[128,1024]{1,0:T(8,128)(2,1)S(1)}, u32[]{:S(2)}, u32[]{:S(2)}) collective-permute-start(bf16[128,1024]{1,0:T(8,128)(2,1)S(1)} %get-tuple-element.110), channel_id=1, source_target_pairs={{32,0},{33,1},{34,2},{35,3},{36,4},{37,5},{38,6},{39,7},{40,8},{41... | collective-permute-start | bytes 786440 | tf_op jit(solution)/shard_map/ppermute | solution.py:575
  30.6 7.9 %collective-permute-start.4 = (bf16[128,1024]{1,0:T(8,128)(2,1)S(1)}, bf16[128,1024]{1,0:T(8,128)(2,1)S(1)}, u32[]{:S(2)}, u32[]{:S(2)}) collective-permute-start(bf16[128,1024]{1,0:T(8,128)(2,1)S(1)} %get-tuple-element.111), channel_id=1, source_target_pairs={{48,0},{49,1},{50,2},{51,3},{52,4},{53,5},{54,6},{55,7},{56,8},{57... | collective-permute-start | bytes 786440 | tf_op jit(solution)/shard_map/ppermute | solution.py:575
  31.9 53.5 %copy-start.7 = (bf16[4096]{0:T(1024)(128)(2,1)S(1)}, bf16[4096]{0:T(1024)(128)(2,1)}, u32[]{:S(2)}) copy-start(bf16[4096]{0:T(1024)(128)(2,1)} %param.19) | copy-start | bytes 24580
  38.5 3.9 collective-permute-start.7
  44.0 6.3 %collective-permute-start.8 = (bf16[128,768]{1,0:T(8,128)(2,1)S(1)}, bf16[128,768]{1,0:T(8,128)(2,1)S(1)}, u32[]{:S(2)}, u32[]{:S(2)}) collective-permute-start(bf16[128,768]{1,0:T(8,128)(2,1)S(1)} %get-tuple-element.67), channel_id=1, source_target_pairs={{16,0},{17,1},{18,2},{19,3},{20,4},{21,5},{22,6},{23,7},{24,8},{25... | collective-permute-start | bytes 589832 | tf_op jit(solution)/shard_map/ppermute | solution.py:575
  45.4 7.3 %collective-permute-start.9 = (bf16[128,768]{1,0:T(8,128)(2,1)S(1)}, bf16[128,768]{1,0:T(8,128)(2,1)S(1)}, u32[]{:S(2)}, u32[]{:S(2)}) collective-permute-start(bf16[128,768]{1,0:T(8,128)(2,1)S(1)} %get-tuple-element.68), channel_id=1, source_target_pairs={{32,0},{33,1},{34,2},{35,3},{36,4},{37,5},{38,6},{39,7},{40,8},{41... | collective-permute-start | bytes 589832 | tf_op jit(solution)/shard_map/ppermute | solution.py:575
  45.9 12.1 %collective-permute-start.10 = (bf16[128,768]{1,0:T(8,128)(2,1)S(1)}, bf16[128,768]{1,0:T(8,128)(2,1)S(1)}, u32[]{:S(2)}, u32[]{:S(2)}) collective-permute-start(bf16[128,768]{1,0:T(8,128)(2,1)S(1)} %get-tuple-element.69), channel_id=1, source_target_pairs={{48,0},{49,1},{50,2},{51,3},{52,4},{53,5},{54,6},{55,7},{56,8},{57... | collective-permute-start | bytes 589832 | tf_op jit(solution)/shard_map/ppermute | solution.py:575
  58.5 4.8 %collective-permute-start.13 = (bf16[128,256]{1,0:T(8,128)(2,1)S(1)}, bf16[128,256]{1,0:T(8,128)(2,1)S(1)}, u32[]{:S(2)}, u32[]{:S(2)}) collective-permute-start(bf16[128,256]{1,0:T(8,128)(2,1)S(1)} %get-tuple-element.81), channel_id=1, source_target_pairs={{66,0},{67,1},{64,2},{65,3},{70,4},{71,5},{68,6},{69,7},{74,8},{75... | collective-permute-start | bytes 196616 | tf_op jit(solution)/shard_map/ppermute | solution.py:575
  58.6 5.4 %collective-permute-start.12 = (bf16[128,256]{1,0:T(8,128)(2,1)S(1)}, bf16[128,256]{1,0:T(8,128)(2,1)S(1)}, u32[]{:S(2)}, u32[]{:S(2)}) collective-permute-start(bf16[128,256]{1,0:T(8,128)(2,1)S(1)} %get-tuple-element.81), channel_id=1, source_target_pairs={{2,0},{3,1},{0,2},{1,3},{6,4},{7,5},{4,6},{5,7},{10,8},{11,9},{8,1... | collective-permute-start | bytes 196616 | tf_op jit(solution)/shard_map/ppermute | solution.py:575
  61.8 3.6 collective-permute-start.11
  61.8 4.1 collective-permute-start.15
  61.8 5.0 %collective-permute-start.14 = (bf16[128,512]{1,0:T(8,128)(2,1)S(1)}, bf16[128,512]{1,0:T(8,128)(2,1)S(1)}, u32[]{:S(2)}, u32[]{:S(2)}) collective-permute-start(bf16[128,512]{1,0:T(8,128)(2,1)S(1)} %get-tuple-element.80.refs_0_), channel_id=1, source_target_pairs={{48,0},{49,1},{50,2},{51,3},{52,4},{53,5},{54,6},{55,7},{56,8},{57... | collective-permute-start | bytes 393224 | tf_op jit(solution)/shard_map/ppermute | solution.py:575
  63.3 15.3 %collective-permute-start.19 = (bf16[128,512]{1,0:T(8,128)(2,1)S(1)}, bf16[128,512]{1,0:T(8,128)(2,1)S(1)}, u32[]{:S(2)}, u32[]{:S(2)}) collective-permute-start(bf16[128,512]{1,0:T(8,128)(2,1)S(1)} %get-tuple-element.80.refs_0_), channel_id=1, source_target_pairs={{32,0},{33,1},{34,2},{35,3},{36,4},{37,5},{38,6},{39,7},{40,8},{41... | collective-permute-start | bytes 393224 | tf_op jit(solution)/shard_map/ppermute | solution.py:575
  66.9 11.6 %collective-permute-start.18 = (bf16[4,128,256]{2,1,0:T(8,128)(2,1)S(1)}, bf16[4,128,256]{2,1,0:T(8,128)(2,1)S(1)}, u32[]{:S(2)}, u32[]{:S(2)}) collective-permute-start(bf16[4,128,256]{2,1,0:T(8,128)(2,1)S(1)} %pad_maximum_fusion), channel_id=1, source_target_pairs={{4,0},{5,1},{6,2},{7,3},{8,4},{9,5},{10,6},{11,7},{12,8},{13,9},{1... | collective-permute-start | bytes 786440 | tf_op jit(solution)/shard_map/ppermute | solution.py:575
  71.2 7.3 %collective-permute-start.17 = (bf16[4,128,256]{2,1,0:T(8,128)(2,1)S(1)}, bf16[4,128,256]{2,1,0:T(8,128)(2,1)S(1)}, u32[]{:S(2)}, u32[]{:S(2)}) collective-permute-start(bf16[4,128,256]{2,1,0:T(8,128)(2,1)S(1)} %pad_maximum_fusion), channel_id=1, source_target_pairs={{8,0},{9,1},{10,2},{11,3},{12,4},{13,5},{14,6},{15,7},{0,8},{1,9},... | collective-permute-start | bytes 786440 | tf_op jit(solution)/shard_map/ppermute | solution.py:575
  71.2 7.0 %collective-permute-start.16 = (bf16[4,128,256]{2,1,0:T(8,128)(2,1)S(1)}, bf16[4,128,256]{2,1,0:T(8,128)(2,1)S(1)}, u32[]{:S(2)}, u32[]{:S(2)}) collective-permute-start(bf16[4,128,256]{2,1,0:T(8,128)(2,1)S(1)} %pad_maximum_fusion), channel_id=1, source_target_pairs={{12,0},{13,1},{14,2},{15,3},{0,4},{1,5},{2,6},{3,7},{4,8},{5,9},{6... | collective-permute-start | bytes 786440 | tf_op jit(solution)/shard_map/ppermute | solution.py:575
  78.6 13.5 %collective-permute-start.20 = (bf16[2048,256]{1,0:T(8,128)(2,1)S(1)}, bf16[2048,256]{1,0:T(8,128)(2,1)S(1)}, u32[]{:S(2)}, u32[]{:S(2)}) collective-permute-start(bf16[2048,256]{1,0:T(8,128)(2,1)S(1)} %bitcast.36), channel_id=1, source_target_pairs={{1,0},{0,1},{3,2},{2,3},{5,4},{4,5},{7,6},{6,7},{9,8},{8,9},{11,10... | collective-permute-start | bytes 3145736 | tf_op jit(solution)/shard_map/ppermute | solution.py:575
  96.7 5.9 %collective-permute-start.21 = (bf16[128,640]{1,0:T(8,128)(2,1)S(1)}, bf16[128,640]{1,0:T(8,128)(2,1)S(1)}, u32[]{:S(2)}, u32[]{:S(2)}) collective-permute-start(bf16[128,640]{1,0:T(8,128)(2,1)S(1)} %get-tuple-element.90), channel_id=1, source_target_pairs={{16,0},{17,1},{18,2},{19,3},{20,4},{21,5},{22,6},{23,7},{24,8},{25... | collective-permute-start | bytes 491528 | tf_op jit(solution)/shard_map/ppermute | solution.py:575
  96.8 7.4 %collective-permute-start.22 = (bf16[128,640]{1,0:T(8,128)(2,1)S(1)}, bf16[128,640]{1,0:T(8,128)(2,1)S(1)}, u32[]{:S(2)}, u32[]{:S(2)}) collective-permute-start(bf16[128,640]{1,0:T(8,128)(2,1)S(1)} %get-tuple-element.91), channel_id=1, source_target_pairs={{32,0},{33,1},{34,2},{35,3},{36,4},{37,5},{38,6},{39,7},{40,8},{41... | collective-permute-start | bytes 491528 | tf_op jit(solution)/shard_map/ppermute | solution.py:575
  98.1 9.9 %collective-permute-start.23 = (bf16[128,640]{1,0:T(8,128)(2,1)S(1)}, bf16[128,640]{1,0:T(8,128)(2,1)S(1)}, u32[]{:S(2)}, u32[]{:S(2)}) collective-permute-start(bf16[128,640]{1,0:T(8,128)(2,1)S(1)} %get-tuple-element.92), channel_id=1, source_target_pairs={{48,0},{49,1},{50,2},{51,3},{52,4},{53,5},{54,6},{55,7},{56,8},{57... | collective-permute-start | bytes 491528 | tf_op jit(solution)/shard_map/ppermute | solution.py:575
  99.8 0.7 copy-start
  102.6 5.4 %copy-start.4 = (bf16[128,640]{1,0:T(8,128)(2,1)}, bf16[128,640]{1,0:T(8,128)(2,1)S(1)}, u32[]{:S(2)}) copy-start(bf16[128,640]{1,0:T(8,128)(2,1)S(1)} %collective-permute-done.21.refs_1_) | copy-start | bytes 491524
  104.2 3.8 copy-start.5
  108.0 0.7 copy-start.6
  117.1 103.2 %all-to-all-start.1 = ((bf16[128,8,3584]{2,1,0:T(8,128)(2,1)}), bf16[128,8,3584]{2,1,0:T(8,128)(2,1)}, u32[]{:S(2)}, u32[]{:S(2)}) async-start(bf16[128,8,3584]{2,1,0:T(8,128)(2,1)} %bitcast.43), calls=%async_computation.1 | async-start | bytes 14680064 | tf_op jit(solution)/shard_map/all_to_all | solution.py:673
  220.2 35.9 %all-to-all-start = ((bf16[128,8,1024]{2,1,0:T(8,128)(2,1)}), bf16[128,8,1024]{2,1,0:T(8,128)(2,1)S(1)}, u32[]{:S(2)}, u32[]{:S(2)}) async-start(bf16[128,8,1024]{2,1,0:T(8,128)(2,1)} %bitcast.42), calls=%async_computation | async-start | bytes 4194304 | tf_op jit(solution)/shard_map/all_to_all | solution.py:673
  256.1 1.3 copy-start.3
  275.1 130.8 %all-to-all-start.2 = ((bf16[128,8,4608]{2,1,0:T(8,128)(2,1)}), bf16[128,8,4608]{2,1,0:T(8,128)(2,1)}, u32[]{:S(2)}, u32[]{:S(2)}) async-start(bf16[128,8,4608]{2,1,0:T(8,128)(2,1)} %bitcast.40), calls=%async_computation.2 | async-start | bytes 18874368 | tf_op jit(solution)/shard_map/all_to_all | solution.py:673
Sparse Core Ops, SparseCore 0:
  9.8 59.0 all-gather.1
